TPU v7x, 32 devices: a whole 2x2x4 slice. The times are simulated.
32 devices in a mesh: head: 4 (over x, core), blk: 8 (over z, y).
Axes of the slice: x: 2, y: 2, z: 4, core: 2. Of those that a mesh axis runs over, the one named last changes fastest.
Arguments:
- query: bfloat16 [4096, 8192], P(('blk', 'head'))
- key: bfloat16 [4096, 1024], P(('blk', 'head'))
- value: bfloat16 [4096, 1024], P(('blk', 'head')), may hold values from -6 to 6
- output_gradient: bfloat16 [4096, 8192], P(('blk', 'head')), may hold values from -6 to 6
- pair_codes: int32 [8, 8, 8], P('blk'), may hold values from 0 to 15
- pair_counts: int32 [8, 8], P('blk'), may hold values from 1 to 8
Outputs:
- attn_out: bfloat16 [4096, 8192], P(('blk', 'head'))
- grad_query: bfloat16 [4096, 8192], P(('blk', 'head'))
- key_gradient: bfloat16 [4096, 1024], P(('blk', 'head'))
- value_gradient: bfloat16 [4096, 1024], P(('blk', 'head'))
All inputs are finite; a program needn't handle non-finite values.
Results may differ from a plain program's by a relative error of at most 0.015.
Values may be sent and summed in bfloat16 or wider, within the bound.
A program may use at most 128 MiB of HBM per device.

v0:
```python
import jax
import jax.numpy as jnp
from jax import lax
from jax.sharding import PartitionSpec as P

QUERY_HEADS = 64
KEY_VALUE_HEADS = 8
HEAD_SIZE = 128
BLOCK = 128


NEGATIVE_FILL = -1e30


def from_behind(block, axis, distance):
    devices = range(lax.axis_size(axis))
    route = [((i - distance) % len(devices), i) for i in devices]
    return lax.ppermute(block, axis, route)


def block_scores(q_blk, k_blk, query_block, key_block, first_step, score_scale):
    scores = (
        jnp.einsum("qhgd,khd->hgqk", q_blk, k_blk, preferred_element_type=jnp.float32) * score_scale
    )
    if first_step:
        rows_at = lax.broadcasted_iota(jnp.int32, scores.shape, 2)
        cols_at = lax.broadcasted_iota(jnp.int32, scores.shape, 3)
        allowed = jnp.logical_or(key_block != query_block, cols_at <= rows_at)
        scores = jnp.where(allowed, scores, NEGATIVE_FILL)
    return scores


def forward_pairs(loop_state, queries, kv_pair, codes, count, first_step, score_scale, nblocks):

    def forward_visit(index, carry):
        best, total, acc = carry
        code = codes[index]
        query_block = code // nblocks
        key_block = code % nblocks
        q_blk = lax.dynamic_slice_in_dim(queries, query_block * BLOCK, BLOCK, 0)
        kv_blk = lax.dynamic_slice_in_dim(kv_pair, key_block * BLOCK, BLOCK, 1)
        scores = block_scores(q_blk, kv_blk[0], query_block, key_block, first_step, score_scale)
        best_old = lax.dynamic_slice_in_dim(best, query_block * BLOCK, BLOCK, 2)
        total_old = lax.dynamic_slice_in_dim(total, query_block * BLOCK, BLOCK, 2)
        acc_old = lax.dynamic_slice_in_dim(acc, query_block * BLOCK, BLOCK, 0)
        best_new = jnp.maximum(best_old, jnp.max(scores, axis=-1))
        factor = jnp.exp(best_old - best_new)
        weights = jnp.exp(scores - best_new[..., None])
        total_new = factor * total_old + jnp.sum(weights, axis=-1)
        mixed = jnp.einsum(
            "hgqk,khd->qhgd",
            weights.astype(jnp.bfloat16),
            kv_blk[1],
            preferred_element_type=jnp.float32,
        )
        acc_new = jnp.transpose(factor, (2, 0, 1))[..., None] * acc_old + mixed
        best = lax.dynamic_update_slice_in_dim(best, best_new, query_block * BLOCK, 2)
        total = lax.dynamic_update_slice_in_dim(total, total_new, query_block * BLOCK, 2)
        acc = lax.dynamic_update_slice_in_dim(acc, acc_new, query_block * BLOCK, 0)
        return (best, total, acc)

    return lax.fori_loop(0, count, forward_visit, loop_state)


def backward_pairs(
    loop_state,
    queries,
    grads,
    kv_pair,
    log_total,
    row_dot,
    codes,
    count,
    first_step,
    score_scale,
    nblocks,
):

    def backward_visit(index, carry):
        query_gradient, kv_grad = carry
        code = codes[index]
        query_block = code // nblocks
        key_block = code % nblocks
        q_blk = lax.dynamic_slice_in_dim(queries, query_block * BLOCK, BLOCK, 0)
        g_blk = lax.dynamic_slice_in_dim(grads, query_block * BLOCK, BLOCK, 0)
        kv_blk = lax.dynamic_slice_in_dim(kv_pair, key_block * BLOCK, BLOCK, 1)
        scores = block_scores(q_blk, kv_blk[0], query_block, key_block, first_step, score_scale)
        lse_blk = lax.dynamic_slice_in_dim(log_total, query_block * BLOCK, BLOCK, 2)
        row_blk = lax.dynamic_slice_in_dim(row_dot, query_block * BLOCK, BLOCK, 2)
        prob = jnp.exp(scores - lse_blk[..., None])
        value_part = jnp.einsum(
            "hgqk,qhgd->khd", prob.astype(jnp.bfloat16), g_blk, preferred_element_type=jnp.float32
        )
        dprob = jnp.einsum("qhgd,khd->hgqk", g_blk, kv_blk[1], preferred_element_type=jnp.float32)
        dscore = (prob * (dprob - row_blk[..., None])).astype(jnp.bfloat16)
        query_part = jnp.einsum(
            "hgqk,khd->qhgd", dscore, kv_blk[0], preferred_element_type=jnp.float32
        )
        key_part = jnp.einsum("hgqk,qhgd->khd", dscore, q_blk, preferred_element_type=jnp.float32)
        old_query = lax.dynamic_slice_in_dim(query_gradient, query_block * BLOCK, BLOCK, 0)
        query_gradient = lax.dynamic_update_slice_in_dim(
            query_gradient, old_query + query_part, query_block * BLOCK, 0
        )
        old_kv = lax.dynamic_slice_in_dim(kv_grad, key_block * BLOCK, BLOCK, 1)
        kv_grad = lax.dynamic_update_slice_in_dim(
            kv_grad, old_kv + jnp.stack((key_part, value_part)), key_block * BLOCK, 1
        )
        return (query_gradient, kv_grad)

    return lax.fori_loop(0, count, backward_visit, loop_state)


def body(query, key, value, output_gradient, pair_codes, pair_counts):
    score_scale = HEAD_SIZE ** (-0.5)
    q_rows, k_rows, v_rows, g_rows = (
        lax.all_to_all(query, "head", split_axis=1, concat_axis=0, tiled=True),
        lax.all_to_all(key, "head", split_axis=1, concat_axis=0, tiled=True),
        lax.all_to_all(value, "head", split_axis=1, concat_axis=0, tiled=True),
        lax.all_to_all(output_gradient, "head", split_axis=1, concat_axis=0, tiled=True),
    )
    row_count_local = q_rows.shape[0]
    kv_local = k_rows.shape[1] // HEAD_SIZE
    device_sharding = QUERY_HEADS // KEY_VALUE_HEADS
    nblocks = row_count_local // BLOCK
    queries = q_rows.reshape(row_count_local, kv_local, device_sharding, HEAD_SIZE)
    grads = g_rows.reshape(row_count_local, kv_local, device_sharding, HEAD_SIZE)
    kv_home = jnp.stack(
        (
            k_rows.reshape(row_count_local, kv_local, HEAD_SIZE),
            v_rows.reshape(row_count_local, kv_local, HEAD_SIZE),
        )
    )
    codes = pair_codes[0]
    counts = pair_counts[0]
    nstep = codes.shape[0]
    loop_state = (
        jnp.full((kv_local, device_sharding, row_count_local), NEGATIVE_FILL, jnp.float32),
        jnp.zeros((kv_local, device_sharding, row_count_local), jnp.float32),
        jnp.zeros((row_count_local, kv_local, device_sharding, HEAD_SIZE), jnp.float32),
    )
    seen = []
    kv_now = kv_home
    for step in range(nstep):
        seen.append(kv_now)
        loop_state = forward_pairs(
            loop_state, queries, kv_now, codes[step], counts[step], step == 0, score_scale, nblocks
        )
        if step + 1 < nstep:
            kv_now = from_behind(kv_now, "blk", 1)
    best, total, acc = loop_state
    attn = (acc / jnp.transpose(total, (2, 0, 1))[..., None]).astype(jnp.bfloat16)
    log_total = best + jnp.log(total)
    row_dot = jnp.einsum("qhgd,qhgd->hgq", grads, attn, preferred_element_type=jnp.float32)
    query_gradient = jnp.zeros((row_count_local, kv_local, device_sharding, HEAD_SIZE), jnp.float32)
    empty_key_value = jnp.zeros((2, row_count_local, kv_local, HEAD_SIZE), jnp.float32)
    kv_now = kv_home
    kv_grad = empty_key_value
    for step in range(nstep):
        query_gradient, kv_grad = backward_pairs(
            (query_gradient, kv_grad),
            queries,
            grads,
            kv_now,
            log_total,
            row_dot,
            codes[step],
            counts[step],
            step == 0,
            score_scale,
            nblocks,
        )
        if step + 1 < nstep:
            kv_now = from_behind(kv_now, "blk", 1)
            kv_grad = from_behind(kv_grad, "blk", 1)
    kv_grad = from_behind(kv_grad.astype(jnp.bfloat16), "blk", 1 - nstep).astype(kv_grad.dtype)
    attn_rows = attn.reshape(row_count_local, kv_local * device_sharding * HEAD_SIZE)
    query_rows = (
        (query_gradient * score_scale)
        .astype(jnp.bfloat16)
        .reshape(row_count_local, kv_local * device_sharding * HEAD_SIZE)
    )
    key_rows = (
        (kv_grad[0] * score_scale)
        .astype(jnp.bfloat16)
        .reshape(row_count_local, kv_local * HEAD_SIZE)
    )
    value_rows = kv_grad[1].astype(jnp.bfloat16).reshape(row_count_local, kv_local * HEAD_SIZE)
    attn_out, grad_query, key_gradient, value_gradient = (
        lax.all_to_all(attn_rows, "head", split_axis=0, concat_axis=1, tiled=True),
        lax.all_to_all(query_rows, "head", split_axis=0, concat_axis=1, tiled=True),
        lax.all_to_all(key_rows, "head", split_axis=0, concat_axis=1, tiled=True),
        lax.all_to_all(value_rows, "head", split_axis=0, concat_axis=1, tiled=True),
    )
    return (attn_out, grad_query, key_gradient, value_gradient)


def solution(mesh):
    return jax.shard_map(
        body,
        mesh=mesh,
        in_specs=(
            P(("blk", "head"), None),
            P(("blk", "head"), None),
            P(("blk", "head"), None),
            P(("blk", "head"), None),
            P("blk", None, None),
            P("blk", None),
        ),
        out_specs=(
            P(("blk", "head"), None),
            P(("blk", "head"), None),
            P(("blk", "head"), None),
            P(("blk", "head"), None),
        ),
        check_vma=False,
    )
```

profile of v0, /device:TPU:9, one launch (start us, length us, event | category | flops | bytes accessed | tf_op | source)
XLA Modules:
  0.0 1090.7 jit_solution(17922535047560347177)
XLA Ops:
  2.3 4.0 all-to-all-start
  11.5 4.2 all-to-all-start.1
  20.9 4.4 all-to-all-start.2
  27.2 13.1 %collective-permute-done = bf16[2,512,2,128]{3,2,1,0:T(2,128)(2,1)S(1)} collective-permute-done((bf16[2,512,2,128]{3,2,1,0:T(2,128)(2,1)S(1)}, bf16[2,512,2,128]{3,2,1,0:T(2,128)(2,1)S(1)}, u32[]{:S(2)}, u32[]{:S(2)}) %collective-permute-start) | collective-permute-done | bytes 524320 | tf_op jit(solution)/shard_map/ppermute | solution.py:18
  46.3 7.7 collective-permute-done.1
  55.9 6.2 all-to-all-start.4
  65.7 55.9 %while.240 = (s32[]{:T(128)}, f32[2,8,512]{2,1,0:T(8,128)S(1)}, f32[2,8,512]{2,1,0:T(8,128)S(1)}, f32[512,2,8,128]{0,3,2,1:T(8,128)}, s32[]{:T(128)}, /*index=5*...) while((s32[]{:T(128)}, f32[2,8,512]{2,1,0:T(8,128)S(1)}, ...), condition=%wide.region_3.4_spmd, body=%wide.region_0.3_spmd.sunk | while | flops 137107488 | bytes 6021660 | solution.py:62
  121.7 32.2 %while.241 = (s32[]{:T(128)}, f32[2,8,512]{2,1,0:T(8,128)S(1)}, f32[2,8,512]{2,1,0:T(8,128)S(1)}, f32[512,2,8,128]{0,3,2,1:T(8,128)}, s32[]{:T(128)}, /*index=5*...) while((s32[]{:T(128)}, f32[2,8,512]{2,1,0:T(8,128)S(1)}, ...), condition=%wide.region_7.8_spmd, body=%wide.region_4.7_spmd.sunk | while | flops 136321056 | bytes 6021650 | solution.py:62
  153.9 16.3 %while.242 = (s32[]{:T(128)}, f32[2,8,512]{2,1,0:T(8,128)S(1)}, f32[2,8,512]{2,1,0:T(8,128)S(1)}, f32[512,2,8,128]{0,3,2,1:T(8,128)}, s32[]{:T(128)}, /*index=5*...) while((s32[]{:T(128)}, f32[2,8,512]{2,1,0:T(8,128)S(1)}, ...), condition=%wide.region_11.12_spmd, body=%wide.region_8.11_spmd.sunk | while | flops 136321056 | bytes 6021650 | solution.py:62
  177.6 42.1 %collective-permute-start.3 = (bf16[2,512,2,128]{3,2,1,0:T(2,128)(2,1)}, bf16[2,512,2,128]{3,2,1,0:T(2,128)(2,1)}, u32[]{:S(2)}, u32[]{:S(2)}) collective-permute-start(bf16[2,512,2,128]{3,2,1,0:T(2,128)(2,1)} %collective-permute-done.2), channel_id=1, source_target_pairs={{7,0},{0,1},{1,2},{2,3},{3,4},{4,5},{5,6},{6,7},{15,8},{8,9},{9,10... | collective-permute-start | bytes 1572872 | tf_op jit(solution)/shard_map/ppermute | solution.py:18
  219.8 8.6 while.243
  233.3 12.9 %collective-permute-start.4 = (bf16[2,512,2,128]{3,2,1,0:T(2,128)(2,1)}, bf16[2,512,2,128]{3,2,1,0:T(2,128)(2,1)}, u32[]{:S(2)}, u32[]{:S(2)}) collective-permute-start(bf16[2,512,2,128]{3,2,1,0:T(2,128)(2,1)} %collective-permute-done.3), channel_id=1, source_target_pairs={{7,0},{0,1},{1,2},{2,3},{3,4},{4,5},{5,6},{6,7},{15,8},{8,9},{9,10... | collective-permute-start | bytes 1572872 | tf_op jit(solution)/shard_map/ppermute | solution.py:18
  246.2 32.3 %while.244 = (s32[]{:T(128)}, f32[2,8,512]{2,1,0:T(8,128)S(1)}, f32[2,8,512]{2,1,0:T(8,128)S(1)}, f32[512,2,8,128]{0,3,2,1:T(8,128)}, s32[]{:T(128)}, /*index=5*...) while((s32[]{:T(128)}, f32[2,8,512]{2,1,0:T(8,128)S(1)}, ...), condition=%wide.region_19.20_spmd, body=%wide.region_16.19_spmd.sunk | while | flops 136321056 | bytes 6021650 | solution.py:62
  280.4 32.6 %while.245 = (s32[]{:T(128)}, f32[2,8,512]{2,1,0:T(8,128)S(1)}, f32[2,8,512]{2,1,0:T(8,128)S(1)}, f32[512,2,8,128]{0,3,2,1:T(8,128)}, s32[]{:T(128)}, /*index=5*...) while((s32[]{:T(128)}, f32[2,8,512]{2,1,0:T(8,128)S(1)}, ...), condition=%wide.region_23.24_spmd, body=%wide.region_20.23_spmd.sunk | while | flops 136321056 | bytes 6021650 | solution.py:62
  314.9 8.5 while.246
  323.5 5.9 collective-permute-done.6
  331.2 32.2 %while.247 = (s32[]{:T(128)}, f32[2,8,512]{2,1,0:T(8,128)S(1)}, f32[2,8,512]{2,1,0:T(8,128)S(1)}, f32[512,2,8,128]{0,3,2,1:T(8,128)}, s32[]{:T(128)}, /*index=5*...) while((s32[]{:T(128)}, f32[2,8,512]{2,1,0:T(8,128)S(1)}, ...), condition=%wide.region_31.32_spmd, body=%wide.region_28.31_spmd.sunk | while | flops 136321056 | bytes 6021650 | solution.py:62
  363.4 5.6 bitcast_convert_fusion
  369.0 5.4 copy.531
  374.5 4.3 multiply_reduce_fusion
  382.6 88.8 %while.248 = (s32[]{:T(128)}, f32[512,2,8,128]{0,3,2,1:T(8,128)}, f32[2,512,2,128]{1,3,2,0:T(8,128)}, s32[]{:T(128)}, s32[8]{0:T(128)S(1)}, /*index=5*/bf16[2,51...) while((s32[]{:T(128)}, f32[512,2,8,128]{0,3,2,1:T(8,128)}, ...), condition=%wide.region_33.34_spmd, body=%wide.region_32.33_spmd.sunk | while | flops 338296864 | bytes 10207804 | solution.py:110
  471.4 24.7 %collective-permute-done.7 = f32[2,512,2,128]{1,3,2,0:T(8,128)} collective-permute-done((f32[2,512,2,128]{1,3,2,0:T(8,128)}, f32[2,512,2,128]{1,3,2,0:T(8,128)}, u32[]{:S(2)}, u32[]{:S(2)}) %collective-permute-start.7) | collective-permute-done | bytes 1048608 | tf_op jit(solution)/shard_map/ppermute | solution.py:18
  496.1 51.1 %while.249 = (s32[]{:T(128)}, f32[512,2,8,128]{0,3,2,1:T(8,128)}, f32[2,512,2,128]{1,3,2,0:T(8,128)}, s32[]{:T(128)}, s32[8]{0:T(128)S(1)}, /*index=5*/bf16[2,51...) while((s32[]{:T(128)}, f32[512,2,8,128]{0,3,2,1:T(8,128)}, ...), condition=%wide.region_35.36_spmd, body=%wide.region_34.35_spmd.sunk | while | flops 337510432 | bytes 10207794 | solution.py:110
  547.2 49.7 %collective-permute-start.8 = (f32[2,512,2,128]{1,3,2,0:T(8,128)}, f32[2,512,2,128]{1,3,2,0:T(8,128)}, u32[]{:S(2)}, u32[]{:S(2)}) collective-permute-start(f32[2,512,2,128]{1,3,2,0:T(8,128)} %get-tuple-element.1959), channel_id=1, source_target_pairs={{7,0},{0,1},{1,2},{2,3},{3,4},{4,5},{5,6},{6,7},{15,8},{8,9},{9,10... | collective-permute-start | bytes 3145736 | tf_op jit(solution)/shard_map/ppermute | solution.py:18
  596.9 21.0 %collective-permute-done.8 = f32[2,512,2,128]{1,3,2,0:T(8,128)} collective-permute-done((f32[2,512,2,128]{1,3,2,0:T(8,128)}, f32[2,512,2,128]{1,3,2,0:T(8,128)}, u32[]{:S(2)}, u32[]{:S(2)}) %collective-permute-start.8) | collective-permute-done | bytes 1048608 | tf_op jit(solution)/shard_map/ppermute | solution.py:18
  617.9 25.6 %while.250 = (s32[]{:T(128)}, f32[512,2,8,128]{0,3,2,1:T(8,128)}, f32[2,512,2,128]{1,3,2,0:T(8,128)}, s32[]{:T(128)}, s32[8]{0:T(128)S(1)}, /*index=5*/bf16[2,51...) while((s32[]{:T(128)}, f32[512,2,8,128]{0,3,2,1:T(8,128)}, ...), condition=%wide.region_37.38_spmd, body=%wide.region_36.37_spmd.sunk | while | flops 337510432 | bytes 10207794 | solution.py:110
  643.5 27.3 %collective-permute-start.9 = (f32[2,512,2,128]{1,3,2,0:T(8,128)}, f32[2,512,2,128]{1,3,2,0:T(8,128)}, u32[]{:S(2)}, u32[]{:S(2)}) collective-permute-start(f32[2,512,2,128]{1,3,2,0:T(8,128)} %get-tuple-element.1961), channel_id=1, source_target_pairs={{7,0},{0,1},{1,2},{2,3},{3,4},{4,5},{5,6},{6,7},{15,8},{8,9},{9,10... | collective-permute-start | bytes 3145736 | tf_op jit(solution)/shard_map/ppermute | solution.py:18
  670.8 20.1 %collective-permute-done.9 = f32[2,512,2,128]{1,3,2,0:T(8,128)} collective-permute-done((f32[2,512,2,128]{1,3,2,0:T(8,128)}, f32[2,512,2,128]{1,3,2,0:T(8,128)}, u32[]{:S(2)}, u32[]{:S(2)}) %collective-permute-start.9) | collective-permute-done | bytes 1048608 | tf_op jit(solution)/shard_map/ppermute | solution.py:18
  690.9 13.3 %while.251 = (s32[]{:T(128)}, f32[512,2,8,128]{0,3,2,1:T(8,128)}, f32[2,512,2,128]{1,3,2,0:T(8,128)}, s32[]{:T(128)}, s32[8]{0:T(128)S(1)}, /*index=5*/bf16[2,51...) while((s32[]{:T(128)}, f32[512,2,8,128]{0,3,2,1:T(8,128)}, ...), condition=%wide.region_39.40_spmd, body=%wide.region_38.39_spmd.sunk | while | flops 337510432 | bytes 10207794 | solution.py:110
  704.2 27.5 %collective-permute-start.10 = (f32[2,512,2,128]{1,3,2,0:T(8,128)}, f32[2,512,2,128]{1,3,2,0:T(8,128)}, u32[]{:S(2)}, u32[]{:S(2)}) collective-permute-start(f32[2,512,2,128]{1,3,2,0:T(8,128)} %get-tuple-element.1963), channel_id=1, source_target_pairs={{7,0},{0,1},{1,2},{2,3},{3,4},{4,5},{5,6},{6,7},{15,8},{8,9},{9,10... | collective-permute-start | bytes 3145736 | tf_op jit(solution)/shard_map/ppermute | solution.py:18
  731.8 19.2 %collective-permute-done.10 = f32[2,512,2,128]{1,3,2,0:T(8,128)} collective-permute-done((f32[2,512,2,128]{1,3,2,0:T(8,128)}, f32[2,512,2,128]{1,3,2,0:T(8,128)}, u32[]{:S(2)}, u32[]{:S(2)}) %collective-permute-start.10) | collective-permute-done | bytes 1048608 | tf_op jit(solution)/shard_map/ppermute | solution.py:18
  750.9 50.9 %while.252 = (s32[]{:T(128)}, f32[512,2,8,128]{0,3,2,1:T(8,128)}, f32[2,512,2,128]{1,3,2,0:T(8,128)}, s32[]{:T(128)}, s32[8]{0:T(128)S(1)}, /*index=5*/bf16[2,51...) while((s32[]{:T(128)}, f32[512,2,8,128]{0,3,2,1:T(8,128)}, ...), condition=%wide.region_41.42_spmd, body=%wide.region_40.41_spmd.sunk | while | flops 337510432 | bytes 10207794 | solution.py:110
  803.4 19.8 %collective-permute-done.11 = f32[2,512,2,128]{1,3,2,0:T(8,128)} collective-permute-done((f32[2,512,2,128]{1,3,2,0:T(8,128)}, f32[2,512,2,128]{1,3,2,0:T(8,128)}, u32[]{:S(2)}, u32[]{:S(2)}) %collective-permute-start.11) | collective-permute-done | bytes 1048608 | tf_op jit(solution)/shard_map/ppermute | solution.py:18
  823.3 51.5 %while.253 = (s32[]{:T(128)}, f32[512,2,8,128]{0,3,2,1:T(8,128)}, f32[2,512,2,128]{1,3,2,0:T(8,128)}, s32[]{:T(128)}, s32[8]{0:T(128)S(1)}, /*index=5*/bf16[2,51...) while((s32[]{:T(128)}, f32[512,2,8,128]{0,3,2,1:T(8,128)}, ...), condition=%wide.region_43.44_spmd, body=%wide.region_42.43_spmd.sunk | while | flops 337510432 | bytes 10207794 | solution.py:110
  875.7 19.6 %collective-permute-done.12 = f32[2,512,2,128]{1,3,2,0:T(8,128)} collective-permute-done((f32[2,512,2,128]{1,3,2,0:T(8,128)}, f32[2,512,2,128]{1,3,2,0:T(8,128)}, u32[]{:S(2)}, u32[]{:S(2)}) %collective-permute-start.12) | collective-permute-done | bytes 1048608 | tf_op jit(solution)/shard_map/ppermute | solution.py:18
  895.3 13.2 %while.254 = (s32[]{:T(128)}, f32[512,2,8,128]{0,3,2,1:T(8,128)}, f32[2,512,2,128]{1,3,2,0:T(8,128)}, s32[]{:T(128)}, s32[8]{0:T(128)S(1)}, /*index=5*/bf16[2,51...) while((s32[]{:T(128)}, f32[512,2,8,128]{0,3,2,1:T(8,128)}, ...), condition=%wide.region_45.46_spmd, body=%wide.region_44.45_spmd.sunk | while | flops 337510432 | bytes 10207794 | solution.py:110
  908.5 38.0 %collective-permute-start.13 = (f32[2,512,2,128]{1,3,2,0:T(8,128)}, f32[2,512,2,128]{1,3,2,0:T(8,128)}, u32[]{:S(2)}, u32[]{:S(2)}) collective-permute-start(f32[2,512,2,128]{1,3,2,0:T(8,128)} %get-tuple-element.1969), channel_id=1, source_target_pairs={{7,0},{0,1},{1,2},{2,3},{3,4},{4,5},{5,6},{6,7},{15,8},{8,9},{9,10... | collective-permute-start | bytes 3145736 | tf_op jit(solution)/shard_map/ppermute | solution.py:18
  950.4 4.3 copy.565
  954.7 10.8 all-to-all-start.3
  965.5 50.6 %while.255 = (s32[]{:T(128)}, f32[512,2,8,128]{0,3,2,1:T(8,128)}, f32[2,512,2,128]{1,3,2,0:T(8,128)}, s32[]{:T(128)}, s32[8]{0:T(128)S(1)}, /*index=5*/bf16[2,51...) while((s32[]{:T(128)}, f32[512,2,8,128]{0,3,2,1:T(8,128)}, ...), condition=%wide.region_47.48_spmd, body=%wide.region_46.47_spmd.sunk | while | flops 337510432 | bytes 10207794 | solution.py:110
  1017.5 9.6 collective-permute-done.14
  1028.1 9.0 all-to-all-start.6
  1038.1 4.2 all-to-all-done.6
  1042.3 4.2 all-to-all-start.7
  1051.3 4.4 copy.566
  1063.2 4.1 copy.418
  1069.4 14.8 %all-to-all-done.5 = bf16[4,128,2048]{2,1,0:T(8,128)(2,1)S(1)} async-done(((bf16[4,128,2048]{2,1,0:T(8,128)(2,1)}), bf16[4,128,2048]{2,1,0:T(8,128)(2,1)S(1)}, u32[]{:S(2)}, u32[]{:S(2)}) %all-to-all-start.5) | async-done | bytes 2097184 | tf_op jit(solution)/shard_map/all_to_all | solution.py:190
  1086.7 4.1 copy.419
  (450 shorter events, 449.0 us)
Async XLA Ops:
  2.3 9.2 all-to-all-start
  11.5 9.4 all-to-all-start.1
  20.9 35.0 %all-to-all-start.2 = ((bf16[128,4,2048]{2,0,1:T(8,128)(2,1)}), bf16[128,4,2048]{2,0,1:T(8,128)(2,1)S(1)}, u32[]{:S(2)}, u32[]{:S(2)}) async-start(bf16[128,4,2048]{2,0,1:T(8,128)(2,1)} %bitcast.988), calls=%async_computation.2 | async-start | bytes 4194304 | tf_op jit(solution)/shard_map/all_to_all | solution.py:116
  25.4 18.5 %copy-start.1 = (s32[1,8]{1,0:T(1,128)S(1)}, s32[1,8]{1,0:T(1,128)}, u32[]{:S(2)}) copy-start(s32[1,8]{1,0:T(1,128)} %param.43) | copy-start | bytes 100
  25.4 19.2 %copy-start.2 = (s32[1,8,8]{2,1,0:T(8,128)S(1)}, s32[1,8,8]{2,1,0:T(8,128)}, u32[]{:S(2)}) copy-start(s32[1,8,8]{2,1,0:T(8,128)} %param.42) | copy-start | bytes 772
  25.9 14.4 %collective-permute-start = (bf16[2,512,2,128]{3,2,1,0:T(2,128)(2,1)S(1)}, bf16[2,512,2,128]{3,2,1,0:T(2,128)(2,1)S(1)}, u32[]{:S(2)}, u32[]{:S(2)}) collective-permute-start(bf16[2,512,2,128]{3,2,1,0:T(2,128)(2,1)S(1)} %constant_dynamic-update-slice_fusion.8), channel_id=1, source_target_pairs={{7,0},{0,1},{1,2},{2,3},{3,4},{4,5},{5,6},{6,7},{15,8},{8,9},{9,10... | collective-permute-start | bytes 1572872 | tf_op jit(solution)/shard_map/ppermute | solution.py:18
  40.4 13.6 %collective-permute-start.1 = (bf16[2,512,2,128]{3,2,1,0:T(2,128)(2,1)S(1)}, bf16[2,512,2,128]{3,2,1,0:T(2,128)(2,1)}, u32[]{:S(2)}, u32[]{:S(2)}) collective-permute-start(bf16[2,512,2,128]{3,2,1,0:T(2,128)(2,1)S(1)} %collective-permute-done), channel_id=1, source_target_pairs={{7,0},{0,1},{1,2},{2,3},{3,4},{4,5},{5,6},{6,7},{15,8},{8,9},{9,10... | collective-permute-start | bytes 1572872 | tf_op jit(solution)/shard_map/ppermute | solution.py:18
  55.9 119.8 %collective-permute-start.2 = (bf16[2,512,2,128]{3,2,1,0:T(2,128)(2,1)}, bf16[2,512,2,128]{3,2,1,0:T(2,128)(2,1)}, u32[]{:S(2)}, u32[]{:S(2)}) collective-permute-start(bf16[2,512,2,128]{3,2,1,0:T(2,128)(2,1)} %collective-permute-done.1), channel_id=1, source_target_pairs={{7,0},{0,1},{1,2},{2,3},{3,4},{4,5},{5,6},{6,7},{15,8},{8,9},{9,10... | collective-permute-start | bytes 1572872 | tf_op jit(solution)/shard_map/ppermute | solution.py:18
  55.9 114.3 %all-to-all-start.4 = ((bf16[128,4,2048]{2,0,1:T(8,128)(2,1)}), bf16[128,4,2048]{2,0,1:T(8,128)(2,1)}, u32[]{:S(2)}, u32[]{:S(2)}) async-start(bf16[128,4,2048]{2,0,1:T(8,128)(2,1)} %bitcast.725), calls=%async_computation.4 | async-start | bytes 4194304 | tf_op jit(solution)/shard_map/all_to_all | solution.py:119
  172.4 1.3 copy-start
  177.6 53.8 %collective-permute-start.3 = (bf16[2,512,2,128]{3,2,1,0:T(2,128)(2,1)}, bf16[2,512,2,128]{3,2,1,0:T(2,128)(2,1)}, u32[]{:S(2)}, u32[]{:S(2)}) collective-permute-start(bf16[2,512,2,128]{3,2,1,0:T(2,128)(2,1)} %collective-permute-done.2), channel_id=1, source_target_pairs={{7,0},{0,1},{1,2},{2,3},{3,4},{4,5},{5,6},{6,7},{15,8},{8,9},{9,10... | collective-permute-start | bytes 1572872 | tf_op jit(solution)/shard_map/ppermute | solution.py:18
  233.3 45.2 %collective-permute-start.4 = (bf16[2,512,2,128]{3,2,1,0:T(2,128)(2,1)}, bf16[2,512,2,128]{3,2,1,0:T(2,128)(2,1)}, u32[]{:S(2)}, u32[]{:S(2)}) collective-permute-start(bf16[2,512,2,128]{3,2,1,0:T(2,128)(2,1)} %collective-permute-done.3), channel_id=1, source_target_pairs={{7,0},{0,1},{1,2},{2,3},{3,4},{4,5},{5,6},{6,7},{15,8},{8,9},{9,10... | collective-permute-start | bytes 1572872 | tf_op jit(solution)/shard_map/ppermute | solution.py:18
  280.4 32.6 %collective-permute-start.5 = (bf16[2,512,2,128]{3,2,1,0:T(2,128)(2,1)}, bf16[2,512,2,128]{3,2,1,0:T(2,128)(2,1)}, u32[]{:S(2)}, u32[]{:S(2)}) collective-permute-start(bf16[2,512,2,128]{3,2,1,0:T(2,128)(2,1)} %collective-permute-done.4), channel_id=1, source_target_pairs={{7,0},{0,1},{1,2},{2,3},{3,4},{4,5},{5,6},{6,7},{15,8},{8,9},{9,10... | collective-permute-start | bytes 1572872 | tf_op jit(solution)/shard_map/ppermute | solution.py:18
  314.9 14.4 %collective-permute-start.6 = (bf16[2,512,2,128]{3,2,1,0:T(2,128)(2,1)}, bf16[2,512,2,128]{3,2,1,0:T(2,128)(2,1)}, u32[]{:S(2)}, u32[]{:S(2)}) collective-permute-start(bf16[2,512,2,128]{3,2,1,0:T(2,128)(2,1)} %collective-permute-done.5), channel_id=1, source_target_pairs={{7,0},{0,1},{1,2},{2,3},{3,4},{4,5},{5,6},{6,7},{15,8},{8,9},{9,10... | collective-permute-start | bytes 1572872 | tf_op jit(solution)/shard_map/ppermute | solution.py:18
  471.3 24.8 %collective-permute-start.7 = (f32[2,512,2,128]{1,3,2,0:T(8,128)}, f32[2,512,2,128]{1,3,2,0:T(8,128)}, u32[]{:S(2)}, u32[]{:S(2)}) collective-permute-start(f32[2,512,2,128]{1,3,2,0:T(8,128)} %get-tuple-element.1957), channel_id=1, source_target_pairs={{7,0},{0,1},{1,2},{2,3},{3,4},{4,5},{5,6},{6,7},{15,8},{8,9},{9,10... | collective-permute-start | bytes 3145736 | tf_op jit(solution)/shard_map/ppermute | solution.py:18
  547.2 70.7 %collective-permute-start.8 = (f32[2,512,2,128]{1,3,2,0:T(8,128)}, f32[2,512,2,128]{1,3,2,0:T(8,128)}, u32[]{:S(2)}, u32[]{:S(2)}) collective-permute-start(f32[2,512,2,128]{1,3,2,0:T(8,128)} %get-tuple-element.1959), channel_id=1, source_target_pairs={{7,0},{0,1},{1,2},{2,3},{3,4},{4,5},{5,6},{6,7},{15,8},{8,9},{9,10... | collective-permute-start | bytes 3145736 | tf_op jit(solution)/shard_map/ppermute | solution.py:18
  643.5 47.4 %collective-permute-start.9 = (f32[2,512,2,128]{1,3,2,0:T(8,128)}, f32[2,512,2,128]{1,3,2,0:T(8,128)}, u32[]{:S(2)}, u32[]{:S(2)}) collective-permute-start(f32[2,512,2,128]{1,3,2,0:T(8,128)} %get-tuple-element.1961), channel_id=1, source_target_pairs={{7,0},{0,1},{1,2},{2,3},{3,4},{4,5},{5,6},{6,7},{15,8},{8,9},{9,10... | collective-permute-start | bytes 3145736 | tf_op jit(solution)/shard_map/ppermute | solution.py:18
  704.2 46.7 %collective-permute-start.10 = (f32[2,512,2,128]{1,3,2,0:T(8,128)}, f32[2,512,2,128]{1,3,2,0:T(8,128)}, u32[]{:S(2)}, u32[]{:S(2)}) collective-permute-start(f32[2,512,2,128]{1,3,2,0:T(8,128)} %get-tuple-element.1963), channel_id=1, source_target_pairs={{7,0},{0,1},{1,2},{2,3},{3,4},{4,5},{5,6},{6,7},{15,8},{8,9},{9,10... | collective-permute-start | bytes 3145736 | tf_op jit(solution)/shard_map/ppermute | solution.py:18
  801.9 21.4 %collective-permute-start.11 = (f32[2,512,2,128]{1,3,2,0:T(8,128)}, f32[2,512,2,128]{1,3,2,0:T(8,128)}, u32[]{:S(2)}, u32[]{:S(2)}) collective-permute-start(f32[2,512,2,128]{1,3,2,0:T(8,128)} %get-tuple-element.1965), channel_id=1, source_target_pairs={{7,0},{0,1},{1,2},{2,3},{3,4},{4,5},{5,6},{6,7},{15,8},{8,9},{9,10... | collective-permute-start | bytes 3145736 | tf_op jit(solution)/shard_map/ppermute | solution.py:18
  874.8 20.5 %collective-permute-start.12 = (f32[2,512,2,128]{1,3,2,0:T(8,128)}, f32[2,512,2,128]{1,3,2,0:T(8,128)}, u32[]{:S(2)}, u32[]{:S(2)}) collective-permute-start(f32[2,512,2,128]{1,3,2,0:T(8,128)} %get-tuple-element.1967), channel_id=1, source_target_pairs={{7,0},{0,1},{1,2},{2,3},{3,4},{4,5},{5,6},{6,7},{15,8},{8,9},{9,10... | collective-permute-start | bytes 3145736 | tf_op jit(solution)/shard_map/ppermute | solution.py:18
  908.5 57.0 %collective-permute-start.13 = (f32[2,512,2,128]{1,3,2,0:T(8,128)}, f32[2,512,2,128]{1,3,2,0:T(8,128)}, u32[]{:S(2)}, u32[]{:S(2)}) collective-permute-start(f32[2,512,2,128]{1,3,2,0:T(8,128)} %get-tuple-element.1969), channel_id=1, source_target_pairs={{7,0},{0,1},{1,2},{2,3},{3,4},{4,5},{5,6},{6,7},{15,8},{8,9},{9,10... | collective-permute-start | bytes 3145736 | tf_op jit(solution)/shard_map/ppermute | solution.py:18
  954.7 73.4 %all-to-all-start.3 = ((bf16[4,128,2048]{2,1,0:T(8,128)(2,1)}), bf16[4,128,2048]{2,1,0:T(8,128)(2,1)}, u32[]{:S(2)}, u32[]{:S(2)}) async-start(bf16[4,128,2048]{2,1,0:T(8,128)(2,1)} %copy.565), calls=%async_computation.3 | async-start | bytes 4194304 | tf_op jit(solution)/shard_map/all_to_all | solution.py:189
  1017.4 9.7 collective-permute-start.14
  1028.1 14.2 %all-to-all-start.6 = ((bf16[4,128,256]{2,1,0:T(8,128)(2,1)}), bf16[4,128,256]{2,1,0:T(8,128)(2,1)S(1)}, u32[]{:S(2)}, u32[]{:S(2)}) async-start(bf16[4,128,256]{2,1,0:T(8,128)(2,1)} %copy.567), calls=%async_computation.6 | async-start | bytes 524288 | tf_op jit(solution)/shard_map/all_to_all | solution.py:191
  1042.3 13.4 %all-to-all-start.7 = ((bf16[4,128,256]{2,1,0:T(8,128)(2,1)}), bf16[4,128,256]{2,1,0:T(8,128)(2,1)S(1)}, u32[]{:S(2)}, u32[]{:S(2)}) async-start(bf16[4,128,256]{2,1,0:T(8,128)(2,1)} %copy.568), calls=%async_computation.7 | async-start | bytes 524288 | tf_op jit(solution)/shard_map/all_to_all | solution.py:192
  1055.7 28.4 %all-to-all-start.5 = ((bf16[4,128,2048]{2,1,0:T(8,128)(2,1)}), bf16[4,128,2048]{2,1,0:T(8,128)(2,1)S(1)}, u32[]{:S(2)}, u32[]{:S(2)}) async-start(bf16[4,128,2048]{2,1,0:T(8,128)(2,1)} %copy.566), calls=%async_computation.5 | async-start | bytes 4194304 | tf_op jit(solution)/shard_map/all_to_all | solution.py:190
where the time goes:
time: 1100 us; the launch traced here: 1090 us
  matrix products  292 us (27%)
  starting transfers between devices  248 us (23%)
  waiting for transfers between devices  188 us (17%)
  loops' own time  188 us (17%)
  local copies, waits for them, and re-layouts  108 us (10%)
  other arithmetic  65.7 us (6%)
    ppermute x15, starting transfers between devices, from_behind(): return lax.ppermute(block, axis, route)  202 us
    ppermute x15, waiting for transfers between devices, from_behind(): return lax.ppermute(block, axis, route)  164 us
    another operation x8, loops' own time, backward_pairs(): return lax.fori_loop(0, count, backward_visit, loop_state)  94.4 us
    another operation x8, loops' own time, forward_pairs(): return lax.fori_loop(0, count, forward_visit, loop_state)  94 us
    dot_general x27, matrix products, forward_visit(): jnp.einsum('hgqk,khd->qhgd', weights.astype(jnp.bfloat16), kv_blk[1], pre...  72.3 us
    dot_general x27, matrix products, backward_visit(): jnp.einsum('hgqk,khd->qhgd', dscore, kv_blk[0], preferred_element_type=jn...  72 us
    dot_general x54, matrix products, block_scores(): jnp.einsum('qhgd,khd->hgqk', q_blk, k_blk, preferred_element_type=jnp.flo...  63 us
    dynamic_update_slice x27, other arithmetic, backward_visit(): lax.dynamic_update_slice_in_dim(kv_grad, old_kv + jnp.stack((key_part, va...  46.4 us
  transfers between devices with their start and end apart: 23, of which 15 were waited for; matrix products, arithmetic and copies ran while one was open for 18% of the time, Pallas kernels for 0%

commit v1 on v0

v1 whole, which is shorter than its diff:
```python
import functools
import math

import jax
import jax.numpy as jnp
from jax import lax
from jax.experimental import pallas as pl
from jax.experimental.pallas import tpu as pltpu
from jax.sharding import PartitionSpec as P

KEY_VALUE_HEADS = 8
HEAD_SIZE = 128
BLOCK = 128
NEGATIVE_FILL = -1e30

NT = (((1,), (1,)), ((), ()))
NN = (((1,), (0,)), ((), ()))
TN = (((0,), (0,)), ((), ()))


def dot(a, b, dims):
    return lax.dot_general(a, b, dims, preferred_element_type=jnp.float32)


def attend(
    nstep, nblocks, heads, base_ref, codes_ref, counts_ref,
    q_ref, g_ref, kv_ref, out_ref, dkv_ref,
    lst, cnt, qs, gs, scores, out_t, dq_t, dk, dv,
):
    scale = HEAD_SIZE ** (-0.5)
    c2 = scale * math.log2(math.e)
    qb = pl.program_id(0)
    width = heads * BLOCK

    @pl.when(qb == 0)
    def _():
        dk[...] = jnp.zeros_like(dk)
        dv[...] = jnp.zeros_like(dv)
        base = base_ref[0]
        for b in range(nblocks):
            cnt[b] = 1
            lst[b * nstep * nblocks] = lax.rem(base, nstep) * nblocks + b

        def over_steps(s, _):
            place = lax.rem(base - s + nstep, nstep) * nblocks

            def over_codes(i, _):
                code = codes_ref[s, i]
                row = code // nblocks
                col = code - row * nblocks

                @pl.when(jnp.logical_or(s != 0, row != col))
                def _():
                    n = cnt[row]
                    lst[row * nstep * nblocks + n] = place + col
                    cnt[row] = n + 1

                return 0

            return lax.fori_loop(0, counts_ref[s], over_codes, 0)

        lax.fori_loop(0, nstep, over_steps, 0)

    n = cnt[qb]
    first = qb * nstep * nblocks

    def rows_of(i):
        return pl.ds(pl.multiple_of(lst[first + i] * BLOCK, BLOCK), BLOCK)

    for h in range(heads):
        cols = slice(h * BLOCK, (h + 1) * BLOCK)
        qs[cols, :] = q_ref[:, cols]
        gs[cols, :] = g_ref[:, cols]

    key_at = lax.broadcasted_iota(jnp.int32, (BLOCK, width), 0)
    query_at = lax.broadcasted_iota(jnp.int32, (BLOCK, width), 1) % BLOCK
    s0 = dot(kv_ref[rows_of(0), :HEAD_SIZE], qs[...], NT)
    s0 = jnp.where(key_at <= query_at, s0, NEGATIVE_FILL)
    scores[0] = s0
    top = jnp.max(s0, axis=0, keepdims=True)

    def score_pass(i, top):
        s = dot(kv_ref[rows_of(i), :HEAD_SIZE], qs[...], NT)
        scores[i] = s
        return jnp.maximum(top, jnp.max(s, axis=0, keepdims=True))

    top = lax.fori_loop(1, n, score_pass, top)
    out_t[...] = jnp.zeros_like(out_t)

    def weight_pass(i, total):
        w = jnp.exp2((scores[i] - top) * c2)
        scores[i] = w
        out_t[...] += dot(kv_ref[rows_of(i), HEAD_SIZE:], w.astype(jnp.bfloat16), TN)
        return total + jnp.sum(w, axis=0, keepdims=True)

    total = lax.fori_loop(0, n, weight_pass, jnp.zeros((1, width), jnp.float32))
    inv = 1.0 / total

    row_dots = []
    for h in range(heads):
        cols = slice(h * BLOCK, (h + 1) * BLOCK)
        attn = jnp.transpose(out_t[:, cols] * inv[:, cols]).astype(jnp.bfloat16)
        out_ref[:, cols] = attn
        prod = attn.astype(jnp.float32) * g_ref[:, cols].astype(jnp.float32)
        row_dots.append(jnp.sum(jnp.transpose(prod), axis=0, keepdims=True))
    row_dot = jnp.concatenate(row_dots, axis=1)
    dq_t[...] = jnp.zeros_like(dq_t)

    def grad_pass(i, _):
        rows = rows_of(i)
        p = scores[i] * inv
        dv[rows, :] += dot(p.astype(jnp.bfloat16), gs[...], NN)
        dp = dot(kv_ref[rows, HEAD_SIZE:], gs[...], NT)
        ds = (p * (dp - row_dot)).astype(jnp.bfloat16)
        dk[rows, :] += dot(ds, qs[...], NN)
        dq_t[...] += dot(kv_ref[rows, :HEAD_SIZE], ds, TN)
        return 0

    lax.fori_loop(0, n, grad_pass, 0)
    for h in range(heads):
        cols = slice(h * BLOCK, (h + 1) * BLOCK)
        out_ref[:, width + h * BLOCK : width + (h + 1) * BLOCK] = jnp.transpose(
            dq_t[:, cols] * scale
        ).astype(jnp.bfloat16)

    @pl.when(qb == nblocks - 1)
    def _():
        dkv_ref[:, :HEAD_SIZE] = (dk[...] * scale).astype(jnp.bfloat16)
        dkv_ref[:, HEAD_SIZE:] = dv[...].astype(jnp.bfloat16)


def attention(base, codes, counts, qg, kv):
    nstep = codes.shape[0]
    rows, both = qg.shape
    width = both // 2
    heads = width // HEAD_SIZE
    nblocks = rows // BLOCK
    keys = kv.shape[0]
    f32, bf16 = jnp.float32, jnp.bfloat16
    flops = 6 * 2 * 30 * width * BLOCK * HEAD_SIZE
    return pl.pallas_call(
        functools.partial(attend, nstep, nblocks, heads),
        out_shape=(
            jax.ShapeDtypeStruct((rows, 2 * width), bf16),
            jax.ShapeDtypeStruct((keys, 2 * HEAD_SIZE), bf16),
        ),
        grid_spec=pltpu.PrefetchScalarGridSpec(
            num_scalar_prefetch=3,
            grid=(nblocks,),
            in_specs=[
                pl.BlockSpec((BLOCK, width), lambda i, *_: (i, 0)),
                pl.BlockSpec((BLOCK, width), lambda i, *_: (i, 1)),
                pl.BlockSpec((keys, 2 * HEAD_SIZE), lambda i, *_: (0, 0)),
            ],
            out_specs=[
                pl.BlockSpec((BLOCK, 2 * width), lambda i, *_: (i, 0)),
                pl.BlockSpec((keys, 2 * HEAD_SIZE), lambda i, *_: (0, 0)),
            ],
            scratch_shapes=[
                pltpu.SMEM((nblocks * nstep * nblocks,), jnp.int32),
                pltpu.SMEM((nblocks,), jnp.int32),
                pltpu.VMEM((width, HEAD_SIZE), bf16),
                pltpu.VMEM((width, HEAD_SIZE), bf16),
                pltpu.VMEM((nstep * nblocks, BLOCK, width), f32),
                pltpu.VMEM((HEAD_SIZE, width), f32),
                pltpu.VMEM((HEAD_SIZE, width), f32),
                pltpu.VMEM((keys, HEAD_SIZE), f32),
                pltpu.VMEM((keys, HEAD_SIZE), f32),
            ],
        ),
        compiler_params=pltpu.CompilerParams(vmem_limit_bytes=44 * 2**20),
        cost_estimate=pl.CostEstimate(
            flops=4 * flops, bytes_accessed=2**23, transcendentals=30 * width * BLOCK
        ),
    )(base, codes, counts, qg, qg, kv)


def permuted(block, axis, distance):
    size = lax.axis_size(axis)
    return lax.ppermute(block, axis, [(i, (i + distance) % size) for i in range(size)])


def body(query, key, value, output_gradient, pair_codes, pair_counts):
    rows = query.shape[0]
    nh = lax.axis_size("head")
    nblk = lax.axis_size("blk")
    kv_local = KEY_VALUE_HEADS // nh
    codes, counts = pair_codes[0], pair_counts[0]
    nstep = codes.shape[0]
    whole = nblk == nstep

    def swap(x):
        return lax.all_to_all(x, "head", split_axis=0, concat_axis=0, tiled=True)

    def per_head(x):
        return jnp.transpose(x.reshape(rows, nh, kv_local, -1), (2, 1, 0, 3))

    k_parts, v_parts, q_parts, g_parts = map(per_head, (key, value, query, output_gradient))
    kv = jnp.concatenate([k_parts, v_parts], axis=-1)
    kv = swap(jnp.transpose(kv, (1, 0, 2, 3)))
    qg = [
        swap(jnp.concatenate([q_parts[j], g_parts[j]], axis=-1)).reshape(nh * rows, -1)
        for j in range(kv_local)
    ]

    def window(block):
        if whole:
            return lax.all_gather(block, "blk", axis=0, tiled=True)
        return jnp.concatenate(
            [block] + [permuted(block, "blk", nstep - i) for i in range(1, nstep)], axis=0
        )

    def returned(grads):
        if whole:
            return lax.psum_scatter(grads, "blk", scatter_dimension=0, tiled=True)
        parts = grads.reshape(nstep, nh * rows, -1)
        total = parts[0].astype(jnp.float32)
        for i in range(1, nstep):
            total += permuted(parts[i], "blk", i - nstep).astype(jnp.float32)
        return total.astype(jnp.bfloat16)

    base = lax.axis_index("blk") if whole else jnp.int32(0)
    base = jnp.reshape(base, (1,)).astype(jnp.int32)
    outs, kv_grads = [], []
    for j in range(kv_local):
        home = kv[:, j].reshape(nh * rows, 2 * HEAD_SIZE)
        out, grads = attention(base, codes, counts, qg[j], window(home))
        outs.append(swap(out.reshape(nh, rows, -1)))
        kv_grads.append(returned(grads).reshape(nh, rows, 2, HEAD_SIZE))
    kv_grads = swap(jnp.stack(kv_grads, axis=1))

    def whole_rows(parts, width):
        return jnp.transpose(parts, (2, 0, 1, 3)).reshape(rows, width)

    width = query.shape[1]
    half = width // KEY_VALUE_HEADS
    outs = jnp.stack(outs, axis=1)
    attn_out = whole_rows(outs[..., :half], width)
    grad_query = whole_rows(outs[..., half:], width)
    key_gradient = whole_rows(kv_grads[..., 0, :], key.shape[1])
    value_gradient = whole_rows(kv_grads[..., 1, :], key.shape[1])
    return (attn_out, grad_query, key_gradient, value_gradient)


def solution(mesh):
    tokens = P(("blk", "head"), None)
    return jax.shard_map(
        body,
        mesh=mesh,
        in_specs=(tokens,) * 4 + (P("blk", None, None), P("blk", None)),
        out_specs=(tokens,) * 4,
        check_vma=False,
    )
```

time: 1100 us -> 294 us (0.27)
  matrix products: 292 us -> 0 us
  starting transfers between devices: 248 us -> 15.8 us
  loops' own time: 188 us -> 0 us
  waiting for transfers between devices: 188 us -> 86.4 us
  blocking collectives: 0 us -> 69.4 us
  local copies, waits for them, and re-layouts: 108 us -> 41.8 us
  other arithmetic: 65.7 us -> 6.51 us
  Pallas kernels: 0 us -> 57.6 us
  between operations: 0.95 us -> 13.9 us
    dot_general x189 -> x0, matrix products: 292 us -> none  [the longest x27 72.3 us: forward_visit(): jnp.einsum('hgqk,khd->qhgd', weights.astype(jnp.bfloat16), kv_blk[1], pre...]
    ppermute x15 -> x0, starting transfers between devices: 202 us -> none  [from_behind(): return lax.ppermute(block, axis, route)]
    another operation x16 -> x0, loops' own time: 188 us -> none  [the longest x8 94.4 us: backward_pairs(): return lax.fori_loop(0, count, backward_visit, loop_state)]
    ppermute x15 -> x0, waiting for transfers between devices: 164 us -> none  [from_behind(): return lax.ppermute(block, axis, route)]
    all_to_all x0 -> x3, blocking collectives: none -> 69.4 us  [swap(): return lax.all_to_all(x, 'head', split_axis=0, concat_axis=0, tiled=True)]
    pallas_call x0 -> x2, Pallas kernels: none -> 57.6 us  [attention(): pl.pallas_call(functools.partial(attend, nstep, nblocks, heads), out_shap...]
    reduce_scatter x0 -> x2, waiting for transfers between devices: none -> 57 us  [returned(): return lax.psum_scatter(grads, 'blk', scatter_dimension=0, tiled=True)]
    dynamic_update_slice x54 -> x0, other arithmetic: 46.9 us -> none  [the longest x27 46.4 us: backward_visit(): lax.dynamic_update_slice_in_dim(kv_grad, old_kv + jnp.stack((key_part, va...]
  transfers between devices with their start and end apart: 23 -> 7, of which waited for: 15 -> 3; matrix products, arithmetic and copies ran while one was open for 18% -> 11% of each run, Pallas kernels for 0% -> 20%
where the time goes in v1:
time: 294 us; the launch traced here: 291 us
  waiting for transfers between devices  86.4 us (29%)
  blocking collectives  69.4 us (24%)
  Pallas kernels  57.6 us (20%)
  local copies, waits for them, and re-layouts  41.8 us (14%)
  starting transfers between devices  15.8 us (5%)
  between operations  13.9 us (5%)
  other arithmetic  6.51 us (2%)
    all_to_all x3, blocking collectives, swap(): return lax.all_to_all(x, 'head', split_axis=0, concat_axis=0, tiled=True)  69.4 us
    pallas_call x2, Pallas kernels, attention(): pl.pallas_call(functools.partial(attend, nstep, nblocks, heads), out_shap...  57.6 us
    reduce_scatter x2, waiting for transfers between devices, returned(): return lax.psum_scatter(grads, 'blk', scatter_dimension=0, tiled=True)  57 us
    all_to_all x3, waiting for transfers between devices, swap(): return lax.all_to_all(x, 'head', split_axis=0, concat_axis=0, tiled=True)  24.1 us
    all_to_all x3, starting transfers between devices, swap(): return lax.all_to_all(x, 'head', split_axis=0, concat_axis=0, tiled=True)  15.7 us
    unnamed x26, local copies, waits for them, and re-layouts  14.8 us
    reshape x4, local copies, waits for them, and re-layouts, per_head(): return jnp.transpose(x.reshape(rows, nh, kv_local, -1), (2, 1, 0, 3))  10.2 us
    transpose x5, local copies, waits for them, and re-layouts, whole_rows(): return jnp.transpose(parts, (2, 0, 1, 3)).reshape(rows, width)  6.36 us
  transfers between devices with their start and end apart: 7, of which 3 were waited for; matrix products, arithmetic and copies ran while one was open for 11% of the time, Pallas kernels for 20%

profile of v1, /device:TPU:9, one launch (start us, length us, event | category | flops | bytes accessed | tf_op | source)
XLA Modules:
  0.0 291.4 jit_solution(6027382708228869478)
XLA Ops:
  7.2 0.0 all-gather.3.cloned.1.call-start
  7.2 1.1 copy.53
  8.3 1.1 copy.52
  9.5 0.2 copy.54
  9.7 11.0 %all_to_all.30 = bf16[4,2,128,256]{3,2,1,0:T(8,128)(2,1)S(1)} all-to-all(bf16[4,2,128,256]{3,2,1,0:T(8,128)(2,1)S(1)} %copy.54), channel_id=1, replica_groups=mesh['head'=4,'blk'=8] {'head'}, dimensions={0} | all-to-all | bytes 1048576 | tf_op jit(solution)/shard_map/all_to_all | solution.py:193
  20.8 0.8 fusion.3
  21.6 0.0 all-gather.3.cloned.1.call-update
  21.6 3.3 %reshape.49 = bf16[128,4,2,1024]{3,2,1,0:T(2,128)(2,1)S(1)} reshape(bf16[128,8192]{1,0:T(8,128)(2,1)} %param.9) | data formatting | bytes 4194304 | tf_op jit(solution)/shard_map/reshape | solution.py:196
  24.9 2.5 copy.69
  27.4 3.3 %reshape.48 = bf16[128,4,2,1024]{3,2,1,0:T(2,128)(2,1)S(1)} reshape(bf16[128,8192]{1,0:T(8,128)(2,1)} %param.6) | data formatting | bytes 4194304 | tf_op jit(solution)/shard_map/reshape | solution.py:196
  30.7 1.2 copy.70
  31.9 0.5 copy-done.10
  32.4 1.4 slice_bitcast_fusion
  33.8 1.5 pad_maximum_fusion.1
  35.3 4.7 %all-to-all-start = ((bf16[4,128,2048]{2,1,0:T(8,128)(2,1)}), bf16[4,128,2048]{2,1,0:T(8,128)(2,1)S(1)}, u32[]{:S(2)}, u32[]{:S(2)}) async-start(bf16[4,128,2048]{2,1,0:T(8,128)(2,1)} %pad_maximum_fusion.1), calls=%async_computation | async-start | bytes 4194304 | tf_op jit(solution)/shard_map/all_to_all | solution.py:193
  40.0 0.7 all-gather.5.cloned.1.call-update
  40.8 0.0 reduce-scatter.3.cloned.1.call-start
  40.8 24.0 %all-to-all-done = bf16[4,128,2048]{2,1,0:T(8,128)(2,1)S(1)} async-done(((bf16[4,128,2048]{2,1,0:T(8,128)(2,1)}), bf16[4,128,2048]{2,1,0:T(8,128)(2,1)S(1)}, u32[]{:S(2)}, u32[]{:S(2)}) %all-to-all-start) | async-done | bytes 2097184 | tf_op jit(solution)/shard_map/all_to_all | solution.py:193
  64.9 1.3 copy-done.1
  66.2 4.6 %all-gather.3.cloned.1.call-done.kv_ref = bf16[4096,256]{1,0:T(8,128)(2,1)} async-done(((bf16[512,256]{1,0:T(8,128)(2,1)}), bf16[4096,256]{1,0:T(8,128)(2,1)}) %all-gather.3.cloned.1.call-update) | async-done | bytes 2097168 | tf_op jit(solution)/shard_map/all_gather | solution.py:208
  70.8 1.6 copy-done.2
  72.4 1.6 copy-done.5
  74.0 29.5 %shard_map.93 = (bf16[512,2048]{1,0:T(8,128)(2,1)S(1)}, bf16[4096,256]{1,0:T(8,128)(2,1)}) custom-call(s32[1]{0:T(128)} %bitcast.base_ref, s32[8,8]{1,0:T(8,128)S(1)} %bitcast.57, s32[8]{0:T(128)S(1)} %bitcast.59, bf16[512,2048]{1,0:T(8,128)(2,1)S(1)} %bitcast.53, bf16[512,2048]{1,0:T(8,128)(2,1)S(1)} %bitcast.54, bf16[4096,256]{1,0:T(8,128)(2,1)S(1)} %copy-done.5), custom_call_target="tpu_custom_call" | custom-call | flops 24159191040 | bytes 8388608 | tf_op jit(solution)/shard_map/pallas_call | solution.py:141
  103.5 0.0 reduce-scatter.3.cloned.1.call-update
  103.5 0.0 reduce-scatter.5.cloned.1.call-start
  103.5 1.4 pad_maximum_fusion.2
  105.0 29.7 %all_to_all.31 = bf16[4,128,2048]{2,1,0:T(8,128)(2,1)} all-to-all(bf16[4,128,2048]{2,1,0:T(8,128)(2,1)S(1)} %pad_maximum_fusion.2), channel_id=1, replica_groups=mesh['head'=4,'blk'=8] {'head'}, dimensions={0} | all-to-all | bytes 4194304 | tf_op jit(solution)/shard_map/all_to_all | solution.py:193
  134.7 1.6 copy-done.4
  136.3 1.6 copy-done.6
  137.9 28.1 %shard_map.94 = (bf16[512,2048]{1,0:T(8,128)(2,1)S(1)}, bf16[4096,256]{1,0:T(8,128)(2,1)S(1)}) custom-call(s32[1]{0:T(128)} %bitcast.base_ref, s32[8,8]{1,0:T(8,128)S(1)} %bitcast.58, s32[8]{0:T(128)S(1)} %bitcast.60, bf16[512,2048]{1,0:T(8,128)(2,1)S(1)} %bitcast.55, bf16[512,2048]{1,0:T(8,128)(2,1)S(1)} %bitcast.56, bf16[4096,256]{1,0:T(8,128)(2,1)S(1)} %copy-done.6), custom_call_target="tpu_custom_call" | custom-call | flops 24159191040 | bytes 8388608 | tf_op jit(solution)/shard_map/pallas_call | solution.py:141
  166.0 1.3 copy-done
  167.3 1.4 copy-done.3
  168.7 28.6 %all_to_all.32 = bf16[4,128,2048]{2,1,0:T(8,128)(2,1)} all-to-all(bf16[4,128,2048]{2,1,0:T(8,128)(2,1)S(1)} %bitcast.51), channel_id=1, replica_groups=mesh['head'=4,'blk'=8] {'head'}, dimensions={0} | all-to-all | bytes 4194304 | tf_op jit(solution)/shard_map/all_to_all | solution.py:193
  197.4 5.5 %all-to-all-start.4 = ((bf16[4,128,2048]{2,1,0:T(8,128)(2,1)}), bf16[4,128,2048]{2,1,0:T(8,128)(2,1)}, u32[]{:S(2)}, u32[]{:S(2)}) async-start(bf16[4,128,2048]{2,1,0:T(8,128)(2,1)} %bitcast.52), calls=%async_computation.4 | async-start | bytes 4194304 | tf_op jit(solution)/shard_map/all_to_all | solution.py:193
  202.8 1.2 stack_reshape.6
  204.1 57.0 %reduce-scatter.5.cloned.1.call-done = bf16[512,256]{1,0:T(8,128)(2,1)} async-done(((bf16[4096,256]{1,0:T(8,128)(2,1)}), bf16[512,256]{1,0:T(8,128)(2,1)}) %reduce-scatter.5.cloned.1.call-update) | async-done | bytes 262160 | tf_op jit(solution)/shard_map/reduce_scatter | solution.py:215
  261.0 1.0 stack_reshape.7
  262.1 0.9 pad_maximum_fusion.3
  263.0 5.5 %all-to-all-start.5 = ((bf16[4,2,128,2,128]{4,2,1,3,0:T(8,128)(2,1)}), bf16[4,2,128,2,128]{4,2,1,3,0:T(8,128)(2,1)S(1)}, u32[]{:S(2)}, u32[]{:S(2)}) async-start(bf16[4,2,128,2,128]{4,2,1,3,0:T(8,128)(2,1)} %pad_maximum_fusion.3), calls=%async_computation.7 | async-start | bytes 1048576 | tf_op jit(solution)/shard_map/all_to_all | solution.py:193
  268.5 2.7 fusion.2
  271.2 2.2 copy.55
  273.4 2.8 reshape.56
  276.2 3.8 %copy.56 = bf16[128,4,2,1024]{3,2,1,0:T(2,128)(2,1)S(1)} copy(bf16[128,4,2,1024]{3,0,1,2:T(8,128)(2,1)} %get-tuple-element.24) | data formatting | bytes 4194304 | tf_op jit(solution)/shard_map/transpose | solution.py:233
  280.0 2.8 reshape.57
  282.8 0.2 copy.60
  283.0 0.9 copy.63
  283.9 0.2 copy.62
  284.0 0.9 copy.64
  (24 shorter events, 0.2 us)
Async XLA Ops:
  7.2 63.6 %all-gather.3.cloned.1.call-start = ((), (), s32[]{:S(2)}) async-start(), calls=%async_computation.8 | async-start | bytes 2359296 | tf_op jit(solution)/shard_map/all_gather | solution.py:208
  30.7 1.7 copy-start.10
  35.3 35.5 %copy-start.7 = (s32[1,8,8]{2,1,0:T(8,128)S(1)}, s32[1,8,8]{2,1,0:T(8,128)}, u32[]{:S(2)}) copy-start(s32[1,8,8]{2,1,0:T(8,128)} %param.10) | copy-start | bytes 772
  35.3 35.5 %copy-start.8 = (s32[1,8]{1,0:T(1,128)S(1)}, s32[1,8]{1,0:T(1,128)}, u32[]{:S(2)}) copy-start(s32[1,8]{1,0:T(1,128)} %param.11) | copy-start | bytes 100
  35.3 29.5 %all-to-all-start = ((bf16[4,128,2048]{2,1,0:T(8,128)(2,1)}), bf16[4,128,2048]{2,1,0:T(8,128)(2,1)S(1)}, u32[]{:S(2)}, u32[]{:S(2)}) async-start(bf16[4,128,2048]{2,1,0:T(8,128)(2,1)} %pad_maximum_fusion.1), calls=%async_computation | async-start | bytes 4194304 | tf_op jit(solution)/shard_map/all_to_all | solution.py:193
  40.0 94.6 %all-gather.5.cloned.1.call-start = ((), (), s32[]{:S(2)}) async-start(), calls=%async_computation.9 | async-start | bytes 2359296 | tf_op jit(solution)/shard_map/all_gather | solution.py:208
  40.8 162.1 %reduce-scatter.3.cloned.1.call-start = ((), (), s32[]{:S(2)}) async-start(), calls=%async_computation.10 | async-start | bytes 2359296 | tf_op jit(solution)/shard_map/reduce_scatter | solution.py:215
  64.9 1.3 copy-start.1
  70.8 1.6 copy-start.2
  72.4 1.6 copy-start.5
  103.5 157.6 %reduce-scatter.5.cloned.1.call-start = ((), (), s32[]{:S(2)}) async-start(), calls=%async_computation.11 | async-start | bytes 2359296 | tf_op jit(solution)/shard_map/reduce_scatter | solution.py:215
  134.7 1.6 copy-start.4
  136.3 1.6 copy-start.6
  166.0 1.3 copy-start
  167.3 1.4 copy-start.3
  197.4 65.6 %all-to-all-start.4 = ((bf16[4,128,2048]{2,1,0:T(8,128)(2,1)}), bf16[4,128,2048]{2,1,0:T(8,128)(2,1)}, u32[]{:S(2)}, u32[]{:S(2)}) async-start(bf16[4,128,2048]{2,1,0:T(8,128)(2,1)} %bitcast.52), calls=%async_computation.4 | async-start | bytes 4194304 | tf_op jit(solution)/shard_map/all_to_all | solution.py:193
  202.8 65.7 %copy-start.9 = (bf16[4,128,2048]{2,1,0:T(8,128)(2,1)S(1)}, bf16[4,128,2048]{2,1,0:T(8,128)(2,1)}, u32[]{:S(2)}) copy-start(bf16[4,128,2048]{2,1,0:T(8,128)(2,1)} %all_to_all.32) | copy-start | bytes 6291460
  263.0 19.8 %all-to-all-start.5 = ((bf16[4,2,128,2,128]{4,2,1,3,0:T(8,128)(2,1)}), bf16[4,2,128,2,128]{4,2,1,3,0:T(8,128)(2,1)S(1)}, u32[]{:S(2)}, u32[]{:S(2)}) async-start(bf16[4,2,128,2,128]{4,2,1,3,0:T(8,128)(2,1)} %pad_maximum_fusion.3), calls=%async_computation.7 | async-start | bytes 1048576 | tf_op jit(solution)/shard_map/all_to_all | solution.py:193
Sparse Core Ops, SparseCore 0:
  21.7 49.0 all-gather.2
  73.5 48.0 all-gather.4
  125.7 65.0 reduce-scatter.2
  194.1 66.8 reduce-scatter.4
